TPU v7x, 32 devices: a whole 2x2x4 slice. The times are simulated.
32 devices in a mesh: tok: 8 (over z, x), tp: 4 (over y, core).
Axes of the slice: x: 2, y: 2, z: 4, core: 2. Of those that a mesh axis runs over, the one named last changes fastest.
Arguments:
- tokens: bfloat16 [4096, 8192], P('tok', 'tp'), may hold values from -6 to 6
- frozen_weight: bfloat16 [8192, 2048], P('tp'), may hold values from -0.0625 to 0.0625
- adapter_down_matrices: bfloat16 [64, 8192, 64], P('tok', 'tp'), may hold values from -0.0625 to 0.0625
- adapter_up_matrices: bfloat16 [64, 64, 2048], P('tok', None, 'tp'), may hold values from -0.75 to 0.75
- adapter_per_block: int32 [256], P('tok'), may hold values from 0 to 63, as said below
- slot_per_adapter: int32 [64], replicated, may hold values from 0 to 63, as said below
- rank_per_adapter: int32 [64], replicated, may hold values from 16 to 64
- output_gradient: bfloat16 [4096, 2048], P('tok', 'tp'), may hold values from -6 to 6
Outputs:
- projected: bfloat16 [4096, 2048], P('tok', 'tp')
- token_gradient: bfloat16 [4096, 8192], P('tok', 'tp')
- grad_down: float32 [64, 8192, 64], P('tok', 'tp')
- grad_up: float32 [64, 64, 2048], P('tok', None, 'tp')
Inputs may be any that keep to these rules, and one draw needn't show every extreme that they name: `adapter_per_block`: block b covers tokens b * 16 to (b + 1) * 16 - 1. Among the blocks of one index of tok, at most 8 have adapters stored on any one index of tok (slots k with k // 8 equal), and one index of tok receives exactly 8 such blocks from every index. A permutation: adapter a is stored in slot slot_per_adapter[a] of adapter_down_matrices and adapter_up_matrices.
All inputs are finite; a program needn't handle non-finite values.
Results may differ from a plain program's by a relative error of at most 0.0033.
Values may be sent and summed in bfloat16 or wider, within the bound.
A program may use at most 128 MiB of HBM per device.

v0:
```python
import jax
import jax.numpy as jnp
from jax import lax
from jax.sharding import PartitionSpec as P

ALPHA = 32
BLOCK_TOKENS = 16


def per_device(
    tokens,
    frozen_weight,
    adapter_down_matrices,
    adapter_up_matrices,
    adapter_per_block,
    slot_per_adapter,
    rank_per_adapter,
    output_gradient,
):
    tok_count = lax.axis_size("tok")
    token_rows = tokens.shape[0]
    width_portion = tokens.shape[1]
    column_portion = output_gradient.shape[1]
    block_count = adapter_per_block.shape[0]
    number_adapters = adapter_down_matrices.shape[0]
    rank_ceiling = adapter_down_matrices.shape[2]
    capacity = max(2, 2 * block_count // tok_count)
    storage_position_count = tok_count * capacity
    adapter_total = slot_per_adapter.shape[0]
    weight_cols = frozen_weight
    base_out = lax.psum_scatter(
        lax.dot_general(
            weight_cols, tokens, (((0,), (1,)), ((), ())), preferred_element_type=jnp.float32
        ),
        "tp",
        scatter_dimension=0,
        tiled=True,
    ).T
    adapter_ids = jnp.arange(adapter_total, dtype=jnp.int32)
    matches = adapter_per_block[:, None] == adapter_ids[None, :]
    block_slot = jnp.sum(jnp.where(matches, slot_per_adapter[None, :], 0), axis=1)
    owner_ids = block_slot // number_adapters
    local_index = block_slot % number_adapters
    block_ids = jnp.arange(block_count, dtype=jnp.int32)
    earlier = (owner_ids[:, None] == owner_ids[None, :]) & (block_ids[None, :] < block_ids[:, None])
    position = jnp.sum(earlier.astype(jnp.int32), axis=1)
    destination = owner_ids * capacity + position
    placement = jnp.arange(storage_position_count, dtype=jnp.int32)[:, None] == destination[None, :]
    place_matrix = placement.astype(jnp.bfloat16)
    send_rows = jnp.dot(
        place_matrix,
        tokens.reshape(block_count, BLOCK_TOKENS * width_portion),
        preferred_element_type=jnp.float32,
    ).astype(jnp.bfloat16)
    send_grads = jnp.dot(
        place_matrix,
        output_gradient.reshape(block_count, BLOCK_TOKENS * column_portion),
        preferred_element_type=jnp.float32,
    ).astype(jnp.bfloat16)
    slot_adapter = jnp.sum(jnp.where(placement, local_index[None, :] + 1, 0), axis=1) - 1
    arrived_rows, arrived_grads, arrived_adapter = (
        lax.all_to_all(
            send_rows.reshape(storage_position_count, BLOCK_TOKENS, width_portion),
            "tok",
            split_axis=0,
            concat_axis=0,
            tiled=True,
        ),
        lax.all_to_all(
            send_grads.reshape(storage_position_count, BLOCK_TOKENS, column_portion),
            "tok",
            split_axis=0,
            concat_axis=0,
            tiled=True,
        ),
        lax.all_to_all(slot_adapter, "tok", split_axis=0, concat_axis=0, tiled=True),
    )
    row_total = storage_position_count * BLOCK_TOKENS
    input_row_block = arrived_rows.reshape(row_total, width_portion)
    gradient_row_block = arrived_grads.reshape(row_total, column_portion)
    chosen = arrived_adapter[:, None] == jnp.arange(number_adapters, dtype=jnp.int32)[None, :]
    chosen_rows = jnp.broadcast_to(
        chosen[:, None, :], (storage_position_count, BLOCK_TOKENS, number_adapters)
    ).reshape(row_total, number_adapters)
    chosen_float = chosen_rows.astype(jnp.float32)
    chosen_half = chosen_rows.astype(jnp.bfloat16)
    stored_ids = lax.axis_index("tok") * number_adapters + jnp.arange(
        number_adapters, dtype=jnp.int32
    )
    stored_match = slot_per_adapter[None, :] == stored_ids[:, None]
    stored_rank = jnp.sum(jnp.where(stored_match, rank_per_adapter[None, :], 0), axis=1)
    stored_scale = jnp.where(
        stored_rank > 0, jnp.float32(ALPHA) / jnp.maximum(stored_rank, 1).astype(jnp.float32), 0.0
    )
    row_rank = jnp.sum(jnp.where(chosen_rows, stored_rank[None, :], 0), axis=1)
    scale_per_row = jnp.sum(chosen_float * stored_scale[None, :], axis=1)
    keep_cols = jnp.arange(rank_ceiling, dtype=jnp.int32)[None, :] < row_rank[:, None]
    reduced_every_row = jnp.einsum(
        "ue,meb->umb", input_row_block, adapter_down_matrices, preferred_element_type=jnp.float32
    )
    low_part = jnp.sum(reduced_every_row * chosen_float[:, :, None], axis=1)
    gathered_every_row = jnp.einsum(
        "hs,gbs->hgb", gradient_row_block, adapter_up_matrices, preferred_element_type=jnp.float32
    )
    pull_part = jnp.sum(gathered_every_row * chosen_float[:, :, None], axis=1)
    low_sum, pull_sum = lax.psum((low_part, pull_part), "tp")
    reduced_rows = jnp.where(keep_cols, low_sum, 0.0).astype(jnp.bfloat16)
    reduced_gradient = (scale_per_row[:, None] * jnp.where(keep_cols, pull_sum, 0.0)).astype(
        jnp.bfloat16
    )
    reduced_picked = chosen_half[:, :, None] * reduced_rows[:, None, :]
    gradient_picked = chosen_half[:, :, None] * reduced_gradient[:, None, :]
    adapter_increment = scale_per_row[:, None] * jnp.einsum(
        "hnq,nqs->hs", reduced_picked, adapter_up_matrices, preferred_element_type=jnp.float32
    )
    grad_down = jnp.einsum(
        "rd,rak->adk", input_row_block, gradient_picked, preferred_element_type=jnp.float32
    )
    grad_up = stored_scale[:, None, None] * jnp.einsum(
        "rak,rc->akc", reduced_picked, gradient_row_block, preferred_element_type=jnp.float32
    )
    adapter_output_rows = jnp.einsum(
        "ymf,mcf->yc", gradient_picked, adapter_down_matrices, preferred_element_type=jnp.float32
    )
    delta_back, row_input_gradient = (
        lax.all_to_all(
            adapter_increment.reshape(storage_position_count, BLOCK_TOKENS, column_portion),
            "tok",
            split_axis=0,
            concat_axis=0,
            tiled=True,
        ),
        lax.all_to_all(
            adapter_output_rows.reshape(storage_position_count, BLOCK_TOKENS, width_portion),
            "tok",
            split_axis=0,
            concat_axis=0,
            tiled=True,
        ),
    )
    adapter_input_gradient = jnp.take(row_input_gradient, destination, axis=0)
    mine_delta = jnp.take(delta_back, destination, axis=0)
    projected = (base_out + mine_delta.reshape(token_rows, column_portion)).astype(jnp.bfloat16)
    weight_cols = frozen_weight
    frozen_input_gradient = lax.dot_general(
        lax.all_gather(output_gradient, "tp", axis=1, tiled=True),
        weight_cols,
        (((1,), (1,)), ((), ())),
        preferred_element_type=jnp.float32,
    )
    token_gradient = (
        frozen_input_gradient + adapter_input_gradient.reshape(token_rows, width_portion)
    ).astype(jnp.bfloat16)
    return (projected, token_gradient, grad_down, grad_up)


def solution(mesh):
    return jax.shard_map(
        per_device,
        mesh=mesh,
        in_specs=(
            P("tok", "tp"),
            P("tp", None),
            P("tok", "tp", None),
            P("tok", None, "tp"),
            P("tok"),
            P(),
            P(),
            P("tok", "tp"),
        ),
        out_specs=(P("tok", "tp"), P("tok", "tp"), P("tok", "tp", None), P("tok", None, "tp")),
        check_vma=False,
    )
```

profile of v0, /device:TPU:0, one launch (start us, length us, event | category | flops | bytes accessed | tf_op | source)
XLA Modules:
  0.0 420.2 jit_solution(17631004640806710069)
XLA Ops:
  9.7 7.3 %all-to-all-start = ((s32[8,8,1]{1,2,0:T(1,128)}), s32[8,8,1]{1,2,0:T(1,128)S(1)}, u32[]{:S(2)}, u32[]{:S(2)}) async-start(s32[8,8,1]{1,2,0:T(1,128)} %bitcast.1), calls=%async_computation.1 | async-start | bytes 8192 | tf_op jit(solution)/shard_map/all_to_all | solution.py:76
  16.9 4.2 reshape.240
  21.1 2.9 convolution_convert_fusion
  24.1 4.4 %copy.26 = bf16[8,8,16,2048]{3,2,1,0:T(8,128)(2,1)} copy(bf16[8,8,16,2048]{3,1,2,0:T(8,128)(2,1)S(1)} %bitcast.71) | data formatting | bytes 8388608
  28.5 6.1 %all-to-all-start.1 = ((bf16[64,16,2048]{2,1,0:T(8,128)(2,1)}), bf16[64,16,2048]{2,1,0:T(8,128)(2,1)}, u32[]{:S(2)}, u32[]{:S(2)}) async-start(bf16[64,16,2048]{2,1,0:T(8,128)(2,1)} %bitcast.70), calls=%async_computation.2 | async-start | bytes 8388608 | tf_op jit(solution)/shard_map/all_to_all | solution.py:62
  38.6 88.8 %all-to-all-done.1 = bf16[64,16,2048]{2,1,0:T(8,128)(2,1)} async-done(((bf16[64,16,2048]{2,1,0:T(8,128)(2,1)}), bf16[64,16,2048]{2,1,0:T(8,128)(2,1)}, u32[]{:S(2)}, u32[]{:S(2)}) %all-to-all-start.1) | async-done | bytes 4194336 | tf_op jit(solution)/shard_map/all_to_all | solution.py:62
  127.4 3.6 all-to-all-start.3
  132.4 4.5 %fusion.28 = f32[1024,512]{0,1:S(1)} fusion(bf16[1024,2048]{1,0:T(8,128)(2,1)} %bitcast.2, bf16[2048,512]{0,1:T(8,128)(2,1)S(1)} %bitcast.69), kind=kOutput, calls=%fused_computation.68 | convolution fusion | flops 2147483648 | bytes 8388608
  137.3 15.0 %all-reduce.4 = bf16[1024,64]{0,1:T(8,128)(2,1)S(1)} all-reduce(f32[1024,64]{0,1:T(8,128)S(1)} %multiply_reduce_fusion.1), channel_id=1, replica_groups=mesh['tok'=8,'tp'=4] {'tp'}, use_global_device_ids=true, to_apply=%region_8.9 | all-reduce | flops 65536 | bytes 393216 | tf_op jit(solution)/shard_map/psum | solution.py:106
  152.3 3.1 bitcast_multiply_fusion
  156.9 4.5 %all-to-all-start.2 = ((f32[64,16,512]{2,1,0:T(8,128)}), f32[64,16,512]{2,1,0:T(8,128)}, u32[]{:S(2)}, u32[]{:S(2)}) async-start(f32[64,16,512]{2,1,0:T(8,128)} %bitcast.76), calls=%async_computation.3 | async-start | bytes 4194304 | tf_op jit(solution)/shard_map/all_to_all | solution.py:126
  161.7 2.5 multiply_reduce_fusion
  164.2 34.3 %all-reduce.3.cloned.1.call-done = f32[1024,64]{0,1:T(8,128)} async-done(((f32[1024,64]{0,1:T(8,128)}), f32[1024,64]{0,1:T(8,128)}) %all-reduce.3.cloned.1.call-update) | async-done | bytes 262160 | tf_op jit(solution)/shard_map/psum | solution.py:106
  199.5 5.6 %fusion.3 = f32[1024,2048,1]{1,0,2:T(8,128)} fusion(bf16[8,2048,64]{1,2,0:T(8,128)(2,1)S(1)} %copy-done, bf16[1024,64]{0,1:T(8,128)(2,1)S(1)} %multiply_convert_fusion, bf16[1024,8]{0,1:T(8,128)(2,1)S(1)} %copy-done.6), kind=kOutput, calls=%fused_computation.12 | convolution fusion | flops 2148007936 | bytes 10633216 | tf_op jit(solution)/shard_map/ymf,mcf->yc/dot_general | solution.py:122
  205.1 4.1 all-to-all-done.2
  209.3 5.1 %all-to-all-start.4 = ((f32[64,16,2048]{2,1,0:T(8,128)}), f32[64,16,2048]{2,1,0:T(8,128)}, u32[]{:S(2)}, u32[]{:S(2)}) async-start(f32[64,16,2048]{2,1,0:T(8,128)} %bitcast.72), calls=%async_computation.5 | async-start | bytes 16777216 | tf_op jit(solution)/shard_map/all_to_all | solution.py:133
  214.4 9.8 %fusion.27 = f32[2048,512]{1,0:T(8,128)} fusion(bf16[2048,2048]{1,0:T(8,128)(2,1)} %param.9, bf16[512,2048]{1,0:T(8,128)(2,1)S(1)} %copy-done.2), kind=kOutput, calls=%fused_computation.67 | convolution fusion | flops 4294967296 | bytes 14680064 | tf_op jit(solution)/shard_map/dot_general | solution.py:32
  225.2 1.7 fusion.8
  226.9 6.5 %convolution_bitcast_fusion = f32[8,2048,64]{1,2,0:T(8,128)} fusion(bf16[1024,2048,1]{1,0,2:T(8,128)(2,1)} %bitcast.17, bf16[1024,64]{0,1:T(8,128)(2,1)S(1)} %multiply_convert_fusion, bf16[1024,8]{0,1:T(8,128)(2,1)S(1)} %copy-done.6), kind=kOutput, calls=%fused_computation.7 | convolution fusion | flops 2148007936 | bytes 8536064 | tf_op jit(solution)/shard_map/rd,rak->adk/dot_general | solution.py:116
  233.4 2.8 gather_fusion
  236.6 33.7 %reduce-scatter.2.cloned.1.call-done = f32[512,512]{1,0:T(8,128)} async-done(((f32[2048,512]{1,0:T(8,128)}), f32[512,512]{1,0:T(8,128)}) %reduce-scatter.2.cloned.1.call-update) | async-done | bytes 1048592 | tf_op jit(solution)/shard_map/reduce_scatter | solution.py:31
  272.7 123.7 %all-to-all-done.4 = f32[64,16,2048]{2,1,0:T(8,128)} async-done(((f32[64,16,2048]{2,1,0:T(8,128)}), f32[64,16,2048]{2,1,0:T(8,128)}, u32[]{:S(2)}, u32[]{:S(2)}) %all-to-all-start.4) | async-done | bytes 8388640 | tf_op jit(solution)/shard_map/all_to_all | solution.py:133
  396.4 6.2 %gather_fusion.1 = f32[32,16,2048]{2,1,0:T(8,128)} fusion(f32[64,16,2048]{2,1,0:T(8,128)} %all-to-all-done.4, s32[1024]{0:T(1024)S(1)} %pad_clamp_fusion), kind=kCustom, calls=%fused_computation.1 | custom fusion | bytes 8388736 | tf_op jit(solution)/shard_map/jit(_take)/gather | solution.py:141
  402.5 11.2 %fusion.1 = bf16[512,2048]{1,0:T(8,128)(2,1)} fusion(f32[32,16,2048]{2,1,0:T(8,128)} %gather_fusion.1, bf16[512,2048]{1,0:T(8,128)(2,1)} %all-gather.2.cloned.1.call-done, bf16[2048,2048]{1,0:T(8,128)(2,1)} %param.9, pred[512]{0:T(512)(128)(4,1)S(1)} %broadcast_in_dim.122), kind=kOutput, calls=%fused_computation.6 | convolution fusion | flops 4298113024 | bytes 16777728 | tf_op jit(solution)/shard_map/dot_general | solution.py:145
  (72 shorter events, 14.6 us)
Async XLA Ops:
  7.2 125.3 %copy-start = (bf16[8,2048,64]{1,2,0:T(8,128)(2,1)S(1)}, bf16[8,2048,64]{1,2,0:T(8,128)(2,1)}, u32[]{:S(2)}) copy-start(bf16[8,2048,64]{1,2,0:T(8,128)(2,1)} %param.10) | copy-start | bytes 6291460
  8.2 0.8 copy-start.11
  8.4 0.5 copy-start.9
  9.7 18.8 %all-to-all-start = ((s32[8,8,1]{1,2,0:T(1,128)}), s32[8,8,1]{1,2,0:T(1,128)S(1)}, u32[]{:S(2)}, u32[]{:S(2)}) async-start(s32[8,8,1]{1,2,0:T(1,128)} %bitcast.1), calls=%async_computation.1 | async-start | bytes 8192 | tf_op jit(solution)/shard_map/all_to_all | solution.py:76
  28.5 6.1 %copy-start.3 = (bf16[512,512]{1,0:T(8,128)(2,1)S(1)}, bf16[512,512]{1,0:T(8,128)(2,1)}, u32[]{:S(2)}) copy-start(bf16[512,512]{1,0:T(8,128)(2,1)} %param.15) | copy-start | bytes 1572868
  28.5 98.9 %all-to-all-start.1 = ((bf16[64,16,2048]{2,1,0:T(8,128)(2,1)}), bf16[64,16,2048]{2,1,0:T(8,128)(2,1)}, u32[]{:S(2)}, u32[]{:S(2)}) async-start(bf16[64,16,2048]{2,1,0:T(8,128)(2,1)} %bitcast.70), calls=%async_computation.2 | async-start | bytes 8388608 | tf_op jit(solution)/shard_map/all_to_all | solution.py:62
  34.9 1.9 copy-start.7
  34.9 1.9 copy-start.8
  38.6 98.4 %copy-start.4 = (f32[1024,8]{0,1:T(8,128)}, f32[1024,8]{0,1:T(8,128)S(1)}, u32[]{:S(2)}) copy-start(f32[1024,8]{0,1:T(8,128)S(1)} %convert_element_type.61) | copy-start | bytes 98308
  127.4 29.6 %all-to-all-start.3 = ((bf16[64,16,512]{2,1,0:T(8,128)(2,1)}), bf16[64,16,512]{2,1,0:T(8,128)(2,1)S(1)}, u32[]{:S(2)}, u32[]{:S(2)}) async-start(bf16[64,16,512]{2,1,0:T(8,128)(2,1)} %bitcast.28), calls=%async_computation.4 | async-start | bytes 2097152 | tf_op jit(solution)/shard_map/all_to_all | solution.py:69
  156.9 4.7 %copy-start.5 = (f32[1024,8]{0,1:T(8,128)S(1)}, f32[1024,8]{0,1:T(8,128)}, u32[]{:S(2)}) copy-start(f32[1024,8]{0,1:T(8,128)} %copy-done.4) | copy-start | bytes 98308
  156.9 52.3 %all-to-all-start.2 = ((f32[64,16,512]{2,1,0:T(8,128)}), f32[64,16,512]{2,1,0:T(8,128)}, u32[]{:S(2)}, u32[]{:S(2)}) async-start(f32[64,16,512]{2,1,0:T(8,128)} %bitcast.76), calls=%async_computation.3 | async-start | bytes 4194304 | tf_op jit(solution)/shard_map/all_to_all | solution.py:126
  161.4 37.1 %all-reduce.3.cloned.1.call-start = ((), (), s32[]{:S(2)}) async-start(), calls=%async_computation.8 | async-start | bytes 524288 | tf_op jit(solution)/shard_map/psum | solution.py:106
  161.7 37.8 %copy-start.6 = (bf16[1024,8]{0,1:T(8,128)(2,1)S(1)}, bf16[1024,8]{0,1:T(8,128)(2,1)}, u32[]{:S(2)}) copy-start(bf16[1024,8]{0,1:T(8,128)(2,1)} %convert_element_type.58) | copy-start | bytes 49156
  209.3 5.2 %copy-start.2 = (bf16[512,2048]{1,0:T(8,128)(2,1)S(1)}, bf16[512,2048]{1,0:T(8,128)(2,1)}, u32[]{:S(2)}) copy-start(bf16[512,2048]{1,0:T(8,128)(2,1)} %param.8) | copy-start | bytes 6291460
  209.3 187.1 %all-to-all-start.4 = ((f32[64,16,2048]{2,1,0:T(8,128)}), f32[64,16,2048]{2,1,0:T(8,128)}, u32[]{:S(2)}, u32[]{:S(2)}) async-start(f32[64,16,2048]{2,1,0:T(8,128)} %bitcast.72), calls=%async_computation.5 | async-start | bytes 16777216 | tf_op jit(solution)/shard_map/all_to_all | solution.py:133
  214.4 55.9 %reduce-scatter.2.cloned.1.call-start = ((), (), s32[]{:S(2)}) async-start(), calls=%async_computation.6 | async-start | bytes 5242880 | tf_op jit(solution)/shard_map/reduce_scatter | solution.py:31
  224.2 0.9 copy-start.10
  224.2 0.9 copy-start.12
  224.2 178.3 %all-gather.2.cloned.1.call-start = ((), (), s32[]{:S(2)}) async-start(), calls=%async_computation.7 | async-start | bytes 2621440 | tf_op jit(solution)/shard_map/all_gather | solution.py:146
  402.5 11.2 %copy-start.1 = (bf16[8,2048,64]{1,2,0:T(8,128)(2,1)S(1)}, bf16[8,2048,64]{1,2,0:T(8,128)(2,1)}, u32[]{:S(2)}) copy-start(bf16[8,2048,64]{1,2,0:T(8,128)(2,1)} %param.10) | copy-start | bytes 6291460
Sparse Core Ops, SparseCore 0:
  165.2 33.2 all-reduce.2
  224.4 45.8 reduce-scatter.1
  271.8 22.5 all-gather.1
where the time goes:
time: 421 us; the launch traced here: 420 us
  waiting for transfers between devices  287 us (68%)
  matrix products  48.4 us (11%)
  starting transfers between devices  27.1 us (6%)
  local copies, waits for them, and re-layouts  24 us (6%)
  blocking collectives  15 us (4%)
  between operations  14 us (3%)
  other arithmetic  5.1 us (1%)
    all_to_all x1, waiting for transfers between devices, per_device(): lax.all_to_all(adapter_output_rows.reshape(storage_position_count, BLOCK_...  124 us
    all_to_all x1, waiting for transfers between devices, per_device(): lax.all_to_all(send_rows.reshape(storage_position_count, BLOCK_TOKENS, wi...  88.8 us
    psum x1, waiting for transfers between devices, per_device(): low_sum, pull_sum = lax.psum((low_part, pull_part), 'tp')  34.3 us
    reduce_scatter x1, waiting for transfers between devices, per_device(): lax.psum_scatter(lax.dot_general(weight_cols, tokens, (((0,), (1,)), ((),...  33.7 us
    psum x1, blocking collectives, per_device(): low_sum, pull_sum = lax.psum((low_part, pull_part), 'tp')  15 us
    dot_general x1, matrix products, per_device(): lax.dot_general(lax.all_gather(output_gradient, 'tp', axis=1, tiled=True)...  11.2 us
    dot_general x1, matrix products, per_device(): lax.dot_general(weight_cols, tokens, (((0,), (1,)), ((), ())), preferred_...  9.79 us
  transfers between devices with their start and end apart: 8, of which 6 were waited for; matrix products, arithmetic and copies ran while one was open for 15% of the time, Pallas kernels for 0%

commit v1 on v0

v1 whole, which is shorter than its diff:
```python
import jax
import jax.numpy as jnp
from jax import lax
from jax.sharding import PartitionSpec as P

ALPHA = 32
BLOCK_TOKENS = 16


def exchange(rows, tok_count):
    total, width = rows.shape
    parts = rows.reshape(tok_count, total // tok_count, width)
    return lax.all_to_all(parts, "tok", split_axis=0, concat_axis=0, tiled=True).reshape(
        total, width
    )


def per_device(
    tokens,
    frozen_weight,
    adapter_down_matrices,
    adapter_up_matrices,
    adapter_per_block,
    slot_per_adapter,
    rank_per_adapter,
    output_gradient,
):
    tok_count = lax.axis_size("tok")
    token_rows = tokens.shape[0]
    block_count = adapter_per_block.shape[0]
    number_adapters, width_portion, rank_ceiling = adapter_down_matrices.shape
    capacity = max(2, 2 * block_count // tok_count)
    storage_position_count = tok_count * capacity
    row_total = storage_position_count * BLOCK_TOKENS
    adapter_total = slot_per_adapter.shape[0]
    stacked = number_adapters * rank_ceiling

    adapter_ids = jnp.arange(adapter_total, dtype=jnp.int32)
    matches = adapter_per_block[:, None] == adapter_ids[None, :]
    block_slot = jnp.sum(jnp.where(matches, slot_per_adapter[None, :], 0), axis=1)
    owner_ids = block_slot // number_adapters
    block_ids = jnp.arange(block_count, dtype=jnp.int32)
    earlier = (owner_ids[:, None] == owner_ids[None, :]) & (block_ids[None, :] < block_ids[:, None])
    position = jnp.sum(earlier.astype(jnp.int32), axis=1)
    destination = owner_ids * capacity + position
    within = jnp.arange(BLOCK_TOKENS, dtype=jnp.int32)
    target_row = (destination[:, None] * BLOCK_TOKENS + within[None, :]).reshape(token_rows)
    place = (jnp.arange(row_total, dtype=jnp.int32)[:, None] == target_row[None, :]).astype(
        jnp.bfloat16
    )
    send_grads = jnp.dot(place, output_gradient, preferred_element_type=jnp.float32).astype(
        jnp.bfloat16
    )
    gradient_rows = exchange(send_grads, tok_count)
    everyones = lax.all_gather(block_slot, "tok", axis=0, tiled=False)
    ours = everyones // number_adapters == lax.axis_index("tok")
    before = block_ids[None, :] < block_ids[:, None]
    rank_in_source = jnp.sum((ours[:, None, :] & before[None, :, :]).astype(jnp.int32), axis=2)
    in_slot = ours[:, None, :] & (
        rank_in_source[:, None, :] == jnp.arange(capacity, dtype=jnp.int32)[None, :, None]
    )
    arrived_adapter = (
        jnp.sum(jnp.where(in_slot, everyones[:, None, :] % number_adapters + 1, 0), axis=2) - 1
    ).reshape(storage_position_count)
    send_rows = jnp.dot(place, tokens, preferred_element_type=jnp.float32).astype(jnp.bfloat16)
    input_rows = exchange(send_rows, tok_count)

    base_out = lax.psum_scatter(
        lax.dot_general(
            frozen_weight, tokens, (((0,), (1,)), ((), ())), preferred_element_type=jnp.float32
        ),
        "tp",
        scatter_dimension=0,
        tiled=True,
    ).T
    frozen_input_gradient = lax.dot_general(
        lax.all_gather(output_gradient, "tp", axis=1, tiled=True),
        frozen_weight,
        (((1,), (1,)), ((), ())),
        preferred_element_type=jnp.float32,
    )

    chosen = arrived_adapter[:, None] == jnp.arange(number_adapters, dtype=jnp.int32)[None, :]
    chosen_rows = jnp.broadcast_to(
        chosen[:, None, :], (storage_position_count, BLOCK_TOKENS, number_adapters)
    ).reshape(row_total, number_adapters)
    chosen_float = chosen_rows.astype(jnp.float32)
    chosen_half = chosen_rows.astype(jnp.bfloat16)
    stored_ids = lax.axis_index("tok") * number_adapters + jnp.arange(
        number_adapters, dtype=jnp.int32
    )
    stored_match = slot_per_adapter[None, :] == stored_ids[:, None]
    stored_rank = jnp.sum(jnp.where(stored_match, rank_per_adapter[None, :], 0), axis=1)
    stored_scale = jnp.where(
        stored_rank > 0, jnp.float32(ALPHA) / jnp.maximum(stored_rank, 1).astype(jnp.float32), 0.0
    )
    row_rank = jnp.sum(jnp.where(chosen_rows, stored_rank[None, :], 0), axis=1)
    scale_per_row = jnp.sum(chosen_float * stored_scale[None, :], axis=1)
    keep_cols = jnp.arange(rank_ceiling, dtype=jnp.int32)[None, :] < row_rank[:, None]

    down_stack = adapter_down_matrices.transpose(0, 2, 1).reshape(stacked, width_portion)
    up_stack = adapter_up_matrices.reshape(stacked, adapter_up_matrices.shape[2])

    pull_all = lax.dot_general(
        gradient_rows, up_stack, (((1,), (1,)), ((), ())), preferred_element_type=jnp.float32
    ).reshape(row_total, number_adapters, rank_ceiling)
    pull_sum = lax.psum(jnp.sum(pull_all * chosen_float[:, :, None], axis=1), "tp")
    reduced_gradient = (scale_per_row[:, None] * jnp.where(keep_cols, pull_sum, 0.0)).astype(
        jnp.bfloat16
    )
    gradient_picked = (chosen_half[:, :, None] * reduced_gradient[:, None, :]).reshape(
        row_total, stacked
    )
    adapter_output_rows = jnp.dot(
        gradient_picked, down_stack, preferred_element_type=jnp.float32
    ).astype(jnp.bfloat16)
    adapter_output_rows, frozen_input_gradient = lax.optimization_barrier(
        (adapter_output_rows, frozen_input_gradient)
    )
    rows_back = exchange(adapter_output_rows, tok_count)

    low_all = lax.dot_general(
        input_rows, down_stack, (((1,), (1,)), ((), ())), preferred_element_type=jnp.float32
    ).reshape(row_total, number_adapters, rank_ceiling)
    low_sum = lax.psum(jnp.sum(low_all * chosen_float[:, :, None], axis=1), "tp")
    reduced_rows = jnp.where(keep_cols, low_sum, 0.0).astype(jnp.bfloat16)
    reduced_picked = (chosen_half[:, :, None] * reduced_rows[:, None, :]).reshape(
        row_total, stacked
    )
    adapter_increment = (
        scale_per_row[:, None]
        * jnp.dot(reduced_picked, up_stack, preferred_element_type=jnp.float32)
    ).astype(jnp.bfloat16)
    adapter_increment, rows_back = lax.optimization_barrier((adapter_increment, rows_back))
    delta_back = exchange(adapter_increment, tok_count)

    grad_down = jnp.einsum(
        "rd,rak->adk",
        input_rows,
        gradient_picked.reshape(row_total, number_adapters, rank_ceiling),
        preferred_element_type=jnp.float32,
    )
    grad_up = stored_scale[:, None, None] * lax.dot_general(
        reduced_picked, gradient_rows, (((0,), (0,)), ((), ())), preferred_element_type=jnp.float32
    ).reshape(adapter_up_matrices.shape)

    taken = (((0,), (0,)), ((), ()))
    token_gradient = (
        frozen_input_gradient
        + lax.dot_general(place, rows_back, taken, preferred_element_type=jnp.float32)
    ).astype(jnp.bfloat16)
    projected = (
        base_out + lax.dot_general(place, delta_back, taken, preferred_element_type=jnp.float32)
    ).astype(jnp.bfloat16)
    return (projected, token_gradient, grad_down, grad_up)


def solution(mesh):
    return jax.shard_map(
        per_device,
        mesh=mesh,
        in_specs=(
            P("tok", "tp"),
            P("tp", None),
            P("tok", "tp", None),
            P("tok", None, "tp"),
            P("tok"),
            P(),
            P(),
            P("tok", "tp"),
        ),
        out_specs=(P("tok", "tp"), P("tok", "tp"), P("tok", "tp", None), P("tok", None, "tp")),
        check_vma=False,
    )
```

time: 421 us -> 351 us (0.83)
  waiting for transfers between devices: 287 us -> 140 us
  blocking collectives: 15 us -> 105 us
  local copies, waits for them, and re-layouts: 24 us -> 4.44 us
  matrix products: 48.4 us -> 60.5 us
  starting transfers between devices: 27.1 us -> 22 us
    all_to_all x5 -> x4, waiting for transfers between devices: 218 us -> 93.1 us  [exchange(): lax.all_to_all(parts, 'tok', split_axis=0, concat_axis=0, tiled=True)]
    unnamed x0 -> x1, blocking collectives: none -> 91.1 us
    reduce_scatter x1, waiting for transfers between devices: 33.7 us -> 0.01 us  [per_device(): lax.psum_scatter(lax.dot_general(frozen_weight, tokens, (((0,), (1,)), ((...]
    dot_general x8 -> x11, matrix products: 32.7 us -> 49.9 us  [the longest x1 9.77 us: per_device(): lax.dot_general(frozen_weight, tokens, (((0,), (1,)), ((), ())), preferre...]
    all_gather x1, waiting for transfers between devices: 0.01 us -> 16.7 us  [per_device(): lax.all_gather(output_gradient, 'tp', axis=1, tiled=True)]
    gather x3 -> x0, local copies, waits for them, and re-layouts: 9.31 us -> none  [the longest x1 6.17 us: per_device(): adapter_input_gradient = jnp.take(row_input_gradient, destination, axis=0)]
    psum x1, waiting for transfers between devices: 34.3 us -> 29.4 us  [per_device(): lax.psum(jnp.sum(pull_all * chosen_float[:, :, None], axis=1), 'tp')]
    all_to_all x5 -> x4, starting transfers between devices: 26.6 us -> 21.7 us  [exchange(): lax.all_to_all(parts, 'tok', split_axis=0, concat_axis=0, tiled=True)]
  transfers between devices with their start and end apart: 8 -> 7, of which waited for: 6 -> 5; matrix products, arithmetic and copies ran while one was open for 15% -> 17% of each run, Pallas kernels for 0% -> 0%
where the time goes in v1:
time: 351 us; the launch traced here: 350 us
  waiting for transfers between devices  140 us (40%)
  blocking collectives  105 us (30%)
  matrix products  60.5 us (17%)
  starting transfers between devices  22 us (6%)
  between operations  14.7 us (4%)
  local copies, waits for them, and re-layouts  4.44 us (1%)
    all_to_all x4, waiting for transfers between devices, exchange(): lax.all_to_all(parts, 'tok', split_axis=0, concat_axis=0, tiled=True)  93.1 us
    unnamed x1, blocking collectives  91.1 us
    psum x1, waiting for transfers between devices, per_device(): lax.psum(jnp.sum(pull_all * chosen_float[:, :, None], axis=1), 'tp')  29.4 us
    all_to_all x4, starting transfers between devices, exchange(): lax.all_to_all(parts, 'tok', split_axis=0, concat_axis=0, tiled=True)  21.7 us
    all_gather x1, waiting for transfers between devices, per_device(): lax.all_gather(output_gradient, 'tp', axis=1, tiled=True)  16.7 us
    psum x1, blocking collectives, per_device(): lax.psum(jnp.sum(low_all * chosen_float[:, :, None], axis=1), 'tp')  14.4 us
    dot_general x1, matrix products, per_device(): lax.dot_general(lax.all_gather(output_gradient, 'tp', axis=1, tiled=True)...  10.5 us
    dot_general x1, matrix products, per_device(): lax.dot_general(frozen_weight, tokens, (((0,), (1,)), ((), ())), preferre...  9.77 us
  transfers between devices with their start and end apart: 7, of which 5 were waited for; matrix products, arithmetic and copies ran while one was open for 17% of the time, Pallas kernels for 0%

profile of v1, /device:TPU:0, one launch (start us, length us, event | category | flops | bytes accessed | tf_op | source)
XLA Modules:
  0.0 350.1 jit_solution(1030715078285923612)
XLA Ops:
  8.6 2.7 fusion.8
  11.3 7.3 %all-to-all-start.1 = ((bf16[8,128,512]{2,1,0:T(8,128)(2,1)}), bf16[8,128,512]{2,1,0:T(8,128)(2,1)S(1)}, u32[]{:S(2)}, u32[]{:S(2)}) async-start(bf16[8,128,512]{2,1,0:T(8,128)(2,1)} %bitcast.60), calls=%async_computation.2 | async-start | bytes 2097152 | tf_op jit(solution)/shard_map/all_to_all | solution.py:13
  18.6 4.3 %convolution_convert_fusion = bf16[1024,2048]{1,0:T(8,128)(2,1)} fusion(bf16[512,2048]{1,0:T(8,128)(2,1)S(1)} %copy-done, s32[512]{0:T(512)S(1)} %add.84), kind=kOutput, calls=%fused_computation.2 | convolution fusion | flops 2150105088 | bytes 6293504 | tf_op jit(solution)/shard_map/dot_general | solution.py:65
  22.9 21.4 %all-to-all-done.1 = bf16[8,128,512]{2,1,0:T(8,128)(2,1)S(1)} async-done(((bf16[8,128,512]{2,1,0:T(8,128)(2,1)}), bf16[8,128,512]{2,1,0:T(8,128)(2,1)S(1)}, u32[]{:S(2)}, u32[]{:S(2)}) %all-to-all-start.1) | async-done | bytes 1048608 | tf_op jit(solution)/shard_map/all_to_all | solution.py:13
  44.3 4.7 %all-to-all-start = ((bf16[8,128,2048]{2,1,0:T(8,128)(2,1)}), bf16[8,128,2048]{2,1,0:T(8,128)(2,1)}, u32[]{:S(2)}, u32[]{:S(2)}) async-start(bf16[8,128,2048]{2,1,0:T(8,128)(2,1)} %bitcast.55), calls=%async_computation.1 | async-start | bytes 8388608 | tf_op jit(solution)/shard_map/all_to_all | solution.py:13
  50.6 91.1 %all-reduce = s32[256]{0:T(256)S(1)} all-reduce(s32[256]{0:T(256)S(1)} %dynamic-update-slice), channel_id=2, replica_groups=mesh['tok'=8,'tp'=4] {'tok'}, use_global_device_ids=true, to_apply=%add | all-reduce | flops 256 | bytes 2048
  142.6 2.5 multiply_reduce_fusion
  147.0 29.4 %all-reduce.4.cloned.1.call-done = f32[1024,64]{0,1:T(8,128)} async-done(((f32[1024,64]{0,1:T(8,128)}), f32[1024,64]{0,1:T(8,128)}) %all-reduce.4.cloned.1.call-update) | async-done | bytes 262160 | tf_op jit(solution)/shard_map/psum | solution.py:107
  178.0 5.9 %bitcast_convert_fusion = bf16[1024,2048]{1,0:T(8,128)(2,1)} fusion(bf16[8,2048,64]{1,2,0:T(8,128)(2,1)} %param.10, bf16[1024,64]{0,1:T(8,128)(2,1)S(1)} %multiply_convert_fusion, bf16[1024,8]{0,1:T(8,128)(2,1)S(1)} %convert_element_type.68), kind=kOutput, calls=%fused_computation | convolution fusion | flops 2150105088 | bytes 6438912 | tf_op jit(solution)/shard_map/dot_general | solution.py:114
  183.9 16.7 %all-gather.3.cloned.1.call-done = bf16[512,2048]{1,0:T(8,128)(2,1)} async-done(((bf16[512,512]{1,0:T(8,128)(2,1)}), bf16[512,2048]{1,0:T(8,128)(2,1)}) %all-gather.3.cloned.1.call-update) | async-done | bytes 2097168 | tf_op jit(solution)/shard_map/all_gather | solution.py:77
  200.6 10.5 %fusion.34 = f32[512,2048]{1,0:T(8,128)} fusion(bf16[512,2048]{1,0:T(8,128)(2,1)} %all-gather.3.cloned.1.call-done, bf16[2048,2048]{1,0:T(8,128)(2,1)} %param.9), kind=kOutput, calls=%fused_computation.71 | convolution fusion | flops 4294967296 | bytes 14680064 | tf_op jit(solution)/shard_map/dot_general | solution.py:76
  211.2 5.5 %all-to-all-start.2 = ((bf16[8,128,2048]{2,1,0:T(8,128)(2,1)}), bf16[8,128,2048]{2,1,0:T(8,128)(2,1)}, u32[]{:S(2)}, u32[]{:S(2)}) async-start(bf16[8,128,2048]{2,1,0:T(8,128)(2,1)} %bitcast.56), calls=%async_computation.3 | async-start | bytes 8388608 | tf_op jit(solution)/shard_map/all_to_all | solution.py:13
  216.9 9.8 %fusion.33 = f32[2048,512]{1,0:T(8,128)} fusion(bf16[2048,2048]{1,0:T(8,128)(2,1)} %param.9, bf16[512,2048]{1,0:T(8,128)(2,1)S(1)} %copy-done), kind=kOutput, calls=%fused_computation.70 | convolution fusion | flops 4294967296 | bytes 14680064 | tf_op jit(solution)/shard_map/dot_general | solution.py:69
  227.4 5.3 %multiply_reduce_fusion.1 = f32[1024,64]{0,1:T(8,128)S(1)} fusion(bf16[1024,2048,1]{1,0,2:T(8,128)(2,1)} %bitcast.4, bf16[8,2048,64]{1,2,0:T(8,128)(2,1)} %param.10, f32[1024,8]{0,1:T(8,128)S(1)} %copy-done.4), kind=kOutput, calls=%fused_computation.10 | convolution fusion | flops 2148466688 | bytes 6586368 | tf_op jit(solution)/shard_map/dot_general | solution.py:122
  232.7 14.4 %all-reduce.5 = bf16[1024,64]{0,1:T(8,128)(2,1)S(1)} all-reduce(f32[1024,64]{0,1:T(8,128)S(1)} %multiply_reduce_fusion.1), channel_id=1, replica_groups=mesh['tok'=8,'tp'=4] {'tp'}, use_global_device_ids=true, to_apply=%region_9.10 | all-reduce | flops 65536 | bytes 393216 | tf_op jit(solution)/shard_map/psum | solution.py:125
  247.1 2.8 fusion
  249.9 60.4 %all-to-all-done.2 = bf16[8,128,2048]{2,1,0:T(8,128)(2,1)} async-done(((bf16[8,128,2048]{2,1,0:T(8,128)(2,1)}), bf16[8,128,2048]{2,1,0:T(8,128)(2,1)}, u32[]{:S(2)}, u32[]{:S(2)}) %all-to-all-start.2) | async-done | bytes 4194336 | tf_op jit(solution)/shard_map/all_to_all | solution.py:13
  310.4 4.2 %all-to-all-start.3 = ((bf16[8,128,512]{2,1,0:T(8,128)(2,1)}), bf16[8,128,512]{2,1,0:T(8,128)(2,1)}, u32[]{:S(2)}, u32[]{:S(2)}) async-start(bf16[8,128,512]{2,1,0:T(8,128)(2,1)} %bitcast.59), calls=%async_computation.4 | async-start | bytes 2097152 | tf_op jit(solution)/shard_map/all_to_all | solution.py:13
  314.6 1.7 convolution_multiply_fusion
  316.3 6.7 %convolution_bitcast_fusion = f32[8,2048,64]{1,2,0:T(8,128)} fusion(bf16[1024,2048,1]{1,0,2:T(8,128)(2,1)} %bitcast.4, bf16[1024,64]{0,1:T(8,128)(2,1)S(1)} %copy-done.2, bf16[1024,8]{0,1:T(8,128)(2,1)S(1)} %copy-done.6), kind=kOutput, calls=%fused_computation.3 | convolution fusion | flops 2148007936 | bytes 8536064 | tf_op jit(solution)/shard_map/rd,rak->adk/dot_general | solution.py:137
  323.0 5.9 %add_convert_fusion = bf16[512,2048]{1,0:T(8,128)(2,1)} fusion(f32[512,2048]{1,0:T(8,128)S(1)} %copy-done.10, bf16[1024,2048]{1,0:T(8,128)(2,1)} %bitcast.12, s32[512]{0:T(512)S(1)} %add.84), kind=kOutput, calls=%fused_computation.1 | convolution fusion | flops 2150105088 | bytes 10487808 | tf_op jit(solution)/shard_map/dot_general | solution.py:150
  328.9 11.3 %all-to-all-done.3 = bf16[8,128,512]{2,1,0:T(8,128)(2,1)} async-done(((bf16[8,128,512]{2,1,0:T(8,128)(2,1)}), bf16[8,128,512]{2,1,0:T(8,128)(2,1)}, u32[]{:S(2)}, u32[]{:S(2)}) %all-to-all-start.3) | async-done | bytes 1048608 | tf_op jit(solution)/shard_map/all_to_all | solution.py:13
  340.2 2.3 fusion.13
  342.6 1.0 copy.21
  (63 shorter events, 7.6 us)
Async XLA Ops:
  7.2 11.4 %copy-start = (bf16[512,2048]{1,0:T(8,128)(2,1)S(1)}, bf16[512,2048]{1,0:T(8,128)(2,1)}, u32[]{:S(2)}) copy-start(bf16[512,2048]{1,0:T(8,128)(2,1)} %param.8) | copy-start | bytes 6291460
  11.3 33.0 %all-to-all-start.1 = ((bf16[8,128,512]{2,1,0:T(8,128)(2,1)}), bf16[8,128,512]{2,1,0:T(8,128)(2,1)S(1)}, u32[]{:S(2)}, u32[]{:S(2)}) async-start(bf16[8,128,512]{2,1,0:T(8,128)(2,1)} %bitcast.60), calls=%async_computation.2 | async-start | bytes 2097152 | tf_op jit(solution)/shard_map/all_to_all | solution.py:13
  44.3 4.8 %copy-start.9 = (u32[32]{0:T(128)S(1)}, u32[32]{0:T(128)}, u32[]{:S(2)}) copy-start(u32[32]{0:T(128)} %constant.59) | copy-start | bytes 388
  44.3 166.8 %all-to-all-start = ((bf16[8,128,2048]{2,1,0:T(8,128)(2,1)}), bf16[8,128,2048]{2,1,0:T(8,128)(2,1)}, u32[]{:S(2)}, u32[]{:S(2)}) async-start(bf16[8,128,2048]{2,1,0:T(8,128)(2,1)} %bitcast.55), calls=%async_computation.1 | async-start | bytes 8388608 | tf_op jit(solution)/shard_map/all_to_all | solution.py:13
  49.0 127.4 %all-reduce.4.cloned.1.call-start = ((), (), s32[]{:S(2)}) async-start(), calls=%async_computation.6 | async-start | bytes 524288 | tf_op jit(solution)/shard_map/psum | solution.py:107
  142.6 3.3 copy-start.3
  142.6 3.3 copy-start.7
  142.6 3.3 copy-start.8
  145.2 55.5 %all-gather.3.cloned.1.call-start = ((), (), s32[]{:S(2)}) async-start(), calls=%async_computation.7 | async-start | bytes 2621440 | tf_op jit(solution)/shard_map/all_gather | solution.py:77
  147.0 36.9 %copy-start.5 = (bf16[1024,8]{0,1:T(8,128)(2,1)}, bf16[1024,8]{0,1:T(8,128)(2,1)S(1)}, u32[]{:S(2)}) copy-start(bf16[1024,8]{0,1:T(8,128)(2,1)S(1)} %convert_element_type.68) | copy-start | bytes 49156
  177.4 0.7 copy-start.1
  211.2 99.2 %all-to-all-start.2 = ((bf16[8,128,2048]{2,1,0:T(8,128)(2,1)}), bf16[8,128,2048]{2,1,0:T(8,128)(2,1)}, u32[]{:S(2)}, u32[]{:S(2)}) async-start(bf16[8,128,2048]{2,1,0:T(8,128)(2,1)} %bitcast.56), calls=%async_computation.3 | async-start | bytes 8388608 | tf_op jit(solution)/shard_map/all_to_all | solution.py:13
  216.7 112.2 %reduce-scatter.2.cloned.1.call-start = ((), (), s32[]{:S(2)}) async-start(), calls=%async_computation.5 | async-start | bytes 5242880 | tf_op jit(solution)/shard_map/reduce_scatter | solution.py:68
  226.7 0.8 copy-start.4
  249.9 64.7 %copy-start.6 = (bf16[1024,8]{0,1:T(8,128)(2,1)S(1)}, bf16[1024,8]{0,1:T(8,128)(2,1)}, u32[]{:S(2)}) copy-start(bf16[1024,8]{0,1:T(8,128)(2,1)} %copy-done.5) | copy-start | bytes 49156
  310.4 29.9 %all-to-all-start.3 = ((bf16[8,128,512]{2,1,0:T(8,128)(2,1)}), bf16[8,128,512]{2,1,0:T(8,128)(2,1)}, u32[]{:S(2)}, u32[]{:S(2)}) async-start(bf16[8,128,512]{2,1,0:T(8,128)(2,1)} %bitcast.59), calls=%async_computation.4 | async-start | bytes 2097152 | tf_op jit(solution)/shard_map/all_to_all | solution.py:13
  314.6 1.7 copy-start.2
  316.3 6.7 %copy-start.10 = (f32[512,2048]{1,0:T(8,128)S(1)}, f32[512,2048]{1,0:T(8,128)}, u32[]{:S(2)}) copy-start(f32[512,2048]{1,0:T(8,128)} %fusion.34) | copy-start | bytes 12582916
Sparse Core Ops, SparseCore 0:
  145.3 31.0 all-reduce.3
  178.0 22.5 all-gather.2
  226.8 44.7 reduce-scatter.1

commit v2 on v1

--- a/solution.py
+++ b/solution.py
@@ -39,6 +39,7 @@
     matches = adapter_per_block[:, None] == adapter_ids[None, :]
     block_slot = jnp.sum(jnp.where(matches, slot_per_adapter[None, :], 0), axis=1)
     owner_ids = block_slot // number_adapters
+    local_index = block_slot % number_adapters
     block_ids = jnp.arange(block_count, dtype=jnp.int32)
     earlier = (owner_ids[:, None] == owner_ids[None, :]) & (block_ids[None, :] < block_ids[:, None])
     position = jnp.sum(earlier.astype(jnp.int32), axis=1)
@@ -48,20 +49,32 @@
     place = (jnp.arange(row_total, dtype=jnp.int32)[:, None] == target_row[None, :]).astype(
         jnp.bfloat16
     )
-    send_grads = jnp.dot(place, output_gradient, preferred_element_type=jnp.float32).astype(
-        jnp.bfloat16
+    part_rows = capacity * BLOCK_TOKENS
+    long_rows = part_rows + BLOCK_TOKENS
+    column_portion = output_gradient.shape[1]
+    long_target = (
+        (owner_ids * long_rows + position * BLOCK_TOKENS)[:, None] + within[None, :]
+    ).reshape(token_rows)
+    note_target = owner_ids * long_rows + part_rows
+    notes = jnp.where(
+        position[:, None] == jnp.arange(column_portion, dtype=jnp.int32)[None, :],
+        (local_index + 1)[:, None],
+        0,
+    ).astype(jnp.bfloat16)
+    place_long = (
+        jnp.arange(tok_count * long_rows, dtype=jnp.int32)[:, None]
+        == jnp.concatenate([long_target, note_target])[None, :]
+    ).astype(jnp.bfloat16)
+    send_grads = jnp.dot(
+        place_long,
+        jnp.concatenate([output_gradient, notes], axis=0),
+        preferred_element_type=jnp.float32,
+    ).astype(jnp.bfloat16)
+    arrived = exchange(send_grads, tok_count).reshape(tok_count, long_rows, column_portion)
+    gradient_rows = arrived[:, :part_rows, :].reshape(row_total, column_portion)
+    arrived_adapter = (
+        arrived[:, part_rows, :capacity].astype(jnp.int32).reshape(storage_position_count) - 1
     )
-    gradient_rows = exchange(send_grads, tok_count)
-    everyones = lax.all_gather(block_slot, "tok", axis=0, tiled=False)
-    ours = everyones // number_adapters == lax.axis_index("tok")
-    before = block_ids[None, :] < block_ids[:, None]
-    rank_in_source = jnp.sum((ours[:, None, :] & before[None, :, :]).astype(jnp.int32), axis=2)
-    in_slot = ours[:, None, :] & (
-        rank_in_source[:, None, :] == jnp.arange(capacity, dtype=jnp.int32)[None, :, None]
-    )
-    arrived_adapter = (
-        jnp.sum(jnp.where(in_slot, everyones[:, None, :] % number_adapters + 1, 0), axis=2) - 1
-    ).reshape(storage_position_count)
     send_rows = jnp.dot(place, tokens, preferred_element_type=jnp.float32).astype(jnp.bfloat16)
     input_rows = exchange(send_rows, tok_count)
 

time: 351 us -> 282 us (0.80)
  blocking collectives: 105 us -> 13.8 us
  waiting for transfers between devices: 140 us -> 167 us
    unnamed x1 -> x0, blocking collectives: 91.1 us -> none
    all_to_all x4, waiting for transfers between devices: 93.1 us -> 117 us  [exchange(): lax.all_to_all(parts, 'tok', split_axis=0, concat_axis=0, tiled=True)]
  transfers between devices with their start and end apart: 7 -> 7, of which waited for: 5 -> 6; matrix products, arithmetic and copies ran while one was open for 17% -> 20% of each run, Pallas kernels for 0% -> 0%
where the time goes in v2:
time: 282 us
  waiting for transfers between devices  167 us (59%)
  matrix products  58.8 us (21%)
  starting transfers between devices  20.9 us (7%)
  between operations  14 us (5%)
  blocking collectives  13.8 us (5%)
  local copies, waits for them, and re-layouts  4 us (1%)
  other arithmetic  2.84 us (1%)
    all_to_all x4, waiting for transfers between devices, exchange(): lax.all_to_all(parts, 'tok', split_axis=0, concat_axis=0, tiled=True)  117 us
    psum x1, waiting for transfers between devices, per_device(): lax.psum(jnp.sum(pull_all * chosen_float[:, :, None], axis=1), 'tp')  31.6 us
    all_to_all x4, starting transfers between devices, exchange(): lax.all_to_all(parts, 'tok', split_axis=0, concat_axis=0, tiled=True)  20.6 us
    all_gather x1, waiting for transfers between devices, per_device(): lax.all_gather(output_gradient, 'tp', axis=1, tiled=True)  17.4 us
    psum x1, blocking collectives, per_device(): lax.psum(jnp.sum(low_all * chosen_float[:, :, None], axis=1), 'tp')  13.8 us
    dot_general x1, matrix products, per_device(): lax.dot_general(lax.all_gather(output_gradient, 'tp', axis=1, tiled=True)...  10.5 us
    dot_general x1, matrix products, per_device(): lax.dot_general(frozen_weight, tokens, (((0,), (1,)), ((), ())), preferre...  9.78 us
    dot_general x1, matrix products, per_device(): jnp.einsum('rd,rak->adk', input_rows, gradient_picked.reshape(row_total,...  6.69 us
  transfers between devices with their start and end apart: 7, of which 6 were waited for; matrix products, arithmetic and copies ran while one was open for 20% of the time, Pallas kernels for 0%

profile of v2, /device:TPU:0, one launch (start us, length us, event | category | flops | bytes accessed | tf_op | source)
XLA Modules:
  0.0 281.6 jit_solution(4612230278863051000)
XLA Ops:
  8.6 3.1 %convolution_convert_fusion.1 = bf16[1152,512]{1,0:T(8,128)(2,1)} fusion(s32[544]{0:T(1024)S(1)} %pad_add_fusion, bf16[32,512]{1,0:T(8,128)(2,1)S(1)} %select_convert_fusion.1, bf16[512,512]{1,0:T(8,128)(2,1)} %param.15), kind=kOutput, calls=%fused_computation.4 | convolution fusion | flops 644059136 | bytes 1738880 | tf_op jit(solution)/shard_map/dot_general | solution.py:68
  11.8 7.3 %all-to-all-start = ((bf16[8,144,512]{2,1,0:T(8,128)(2,1)}), bf16[8,144,512]{2,1,0:T(8,128)(2,1)S(1)}, u32[]{:S(2)}, u32[]{:S(2)}) async-start(bf16[8,144,512]{2,1,0:T(8,128)(2,1)} %bitcast.55), calls=%async_computation.1 | async-start | bytes 2359296 | tf_op jit(solution)/shard_map/all_to_all | solution.py:13
  19.2 4.4 %convolution_convert_fusion = bf16[1024,2048]{1,0:T(8,128)(2,1)} fusion(bf16[512,2048]{1,0:T(8,128)(2,1)S(1)} %copy-done, s32[512]{0:T(512)S(1)} %add.122), kind=kOutput, calls=%fused_computation.2 | convolution fusion | flops 2150105088 | bytes 6293504 | tf_op jit(solution)/shard_map/dot_general | solution.py:78
  23.6 24.1 %all-to-all-done = bf16[8,144,512]{2,1,0:T(8,128)(2,1)S(1)} async-done(((bf16[8,144,512]{2,1,0:T(8,128)(2,1)}), bf16[8,144,512]{2,1,0:T(8,128)(2,1)S(1)}, u32[]{:S(2)}, u32[]{:S(2)}) %all-to-all-start) | async-done | bytes 1179680 | tf_op jit(solution)/shard_map/all_to_all | solution.py:13
  47.6 4.5 %all-to-all-start.1 = ((bf16[8,128,2048]{2,1,0:T(8,128)(2,1)}), bf16[8,128,2048]{2,1,0:T(8,128)(2,1)}, u32[]{:S(2)}, u32[]{:S(2)}) async-start(bf16[8,128,2048]{2,1,0:T(8,128)(2,1)} %bitcast.53), calls=%async_computation.2 | async-start | bytes 8388608 | tf_op jit(solution)/shard_map/all_to_all | solution.py:13
  54.5 1.4 multiply_reduce_fusion
  57.7 31.6 %all-reduce.3.cloned.1.call-done = f32[1024,64]{0,1:T(8,128)} async-done(((f32[1024,64]{0,1:T(8,128)}), f32[1024,64]{0,1:T(8,128)}) %all-reduce.3.cloned.1.call-update) | async-done | bytes 262160 | tf_op jit(solution)/shard_map/psum | solution.py:120
  90.3 5.9 %bitcast_convert_fusion = bf16[1024,2048]{1,0:T(8,128)(2,1)} fusion(bf16[8,2048,64]{1,2,0:T(8,128)(2,1)} %param.10, bf16[1024,64]{0,1:T(8,128)(2,1)S(1)} %multiply_convert_fusion, bf16[1024,8]{0,1:T(8,128)(2,1)S(1)} %convert_element_type.80), kind=kOutput, calls=%fused_computation | convolution fusion | flops 2150105088 | bytes 6438912 | tf_op jit(solution)/shard_map/dot_general | solution.py:127
  96.2 17.4 %all-gather.2.cloned.1.call-done = bf16[512,2048]{1,0:T(8,128)(2,1)} async-done(((bf16[512,512]{1,0:T(8,128)(2,1)}), bf16[512,2048]{1,0:T(8,128)(2,1)}) %all-gather.2.cloned.1.call-update) | async-done | bytes 2097168 | tf_op jit(solution)/shard_map/all_gather | solution.py:90
  113.6 10.5 %fusion.35 = f32[512,2048]{1,0:T(8,128)} fusion(bf16[512,2048]{1,0:T(8,128)(2,1)} %all-gather.2.cloned.1.call-done, bf16[2048,2048]{1,0:T(8,128)(2,1)} %param.9), kind=kOutput, calls=%fused_computation.72 | convolution fusion | flops 4294967296 | bytes 14680064 | tf_op jit(solution)/shard_map/dot_general | solution.py:89
  124.1 20.6 %all-to-all-done.1 = bf16[8,128,2048]{2,1,0:T(8,128)(2,1)} async-done(((bf16[8,128,2048]{2,1,0:T(8,128)(2,1)}), bf16[8,128,2048]{2,1,0:T(8,128)(2,1)}, u32[]{:S(2)}, u32[]{:S(2)}) %all-to-all-start.1) | async-done | bytes 4194336 | tf_op jit(solution)/shard_map/all_to_all | solution.py:13
  144.7 4.6 %all-to-all-start.2 = ((bf16[8,128,2048]{2,1,0:T(8,128)(2,1)}), bf16[8,128,2048]{2,1,0:T(8,128)(2,1)}, u32[]{:S(2)}, u32[]{:S(2)}) async-start(bf16[8,128,2048]{2,1,0:T(8,128)(2,1)} %bitcast.54), calls=%async_computation.3 | async-start | bytes 8388608 | tf_op jit(solution)/shard_map/all_to_all | solution.py:13
  149.6 9.8 %fusion.34 = f32[2048,512]{1,0:T(8,128)} fusion(bf16[2048,2048]{1,0:T(8,128)(2,1)} %param.9, bf16[512,2048]{1,0:T(8,128)(2,1)S(1)} %copy-done), kind=kOutput, calls=%fused_computation.71 | convolution fusion | flops 4294967296 | bytes 14680064 | tf_op jit(solution)/shard_map/dot_general | solution.py:82
  159.4 5.3 %multiply_reduce_fusion.1 = f32[1024,64]{0,1:T(8,128)S(1)} fusion(bf16[1024,2048,1]{1,0,2:T(8,128)(2,1)} %bitcast.4, bf16[8,2048,64]{1,2,0:T(8,128)(2,1)} %param.10, f32[1024,8]{0,1:T(8,128)S(1)} %copy-done.3), kind=kOutput, calls=%fused_computation.12 | convolution fusion | flops 2148466688 | bytes 6586368 | tf_op jit(solution)/shard_map/dot_general | solution.py:135
  164.7 13.8 %all-reduce.4 = bf16[1024,64]{0,1:T(8,128)(2,1)S(1)} all-reduce(f32[1024,64]{0,1:T(8,128)S(1)} %multiply_reduce_fusion.1), channel_id=1, replica_groups=mesh['tok'=8,'tp'=4] {'tp'}, use_global_device_ids=true, to_apply=%region_7.8 | all-reduce | flops 65536 | bytes 393216 | tf_op jit(solution)/shard_map/psum | solution.py:138
  178.6 1.8 fusion
  180.4 61.5 %all-to-all-done.2 = bf16[8,128,2048]{2,1,0:T(8,128)(2,1)} async-done(((bf16[8,128,2048]{2,1,0:T(8,128)(2,1)}), bf16[8,128,2048]{2,1,0:T(8,128)(2,1)}, u32[]{:S(2)}, u32[]{:S(2)}) %all-to-all-start.2) | async-done | bytes 4194336 | tf_op jit(solution)/shard_map/all_to_all | solution.py:13
  241.8 4.2 %all-to-all-start.3 = ((bf16[8,128,512]{2,1,0:T(8,128)(2,1)}), bf16[8,128,512]{2,1,0:T(8,128)(2,1)}, u32[]{:S(2)}, u32[]{:S(2)}) async-start(bf16[8,128,512]{2,1,0:T(8,128)(2,1)} %bitcast.58), calls=%async_computation.4 | async-start | bytes 2097152 | tf_op jit(solution)/shard_map/all_to_all | solution.py:13
  246.1 1.7 convolution_multiply_fusion
  247.8 6.7 %convolution_bitcast_fusion = f32[8,2048,64]{1,2,0:T(8,128)} fusion(bf16[1024,2048,1]{1,0,2:T(8,128)(2,1)} %bitcast.4, bf16[1024,64]{0,1:T(8,128)(2,1)S(1)} %multiply_convert_fusion, bf16[1024,8]{0,1:T(8,128)(2,1)S(1)} %convert_element_type.80), kind=kOutput, calls=%fused_computation.3 | convolution fusion | flops 2148007936 | bytes 8536064 | tf_op jit(solution)/shard_map/rd,rak->adk/dot_general | solution.py:150
  254.5 5.9 %add_convert_fusion = bf16[512,2048]{1,0:T(8,128)(2,1)} fusion(f32[512,2048]{1,0:T(8,128)S(1)} %copy-done.8, bf16[1024,2048]{1,0:T(8,128)(2,1)} %bitcast.11, s32[512]{0:T(512)S(1)} %add.122), kind=kOutput, calls=%fused_computation.1 | convolution fusion | flops 2150105088 | bytes 10487808 | tf_op jit(solution)/shard_map/dot_general | solution.py:163
  260.4 11.3 %all-to-all-done.3 = bf16[8,128,512]{2,1,0:T(8,128)(2,1)} async-done(((bf16[8,128,512]{2,1,0:T(8,128)(2,1)}), bf16[8,128,512]{2,1,0:T(8,128)(2,1)}, u32[]{:S(2)}, u32[]{:S(2)}) %all-to-all-start.3) | async-done | bytes 1048608 | tf_op jit(solution)/shard_map/all_to_all | solution.py:13
  271.7 2.3 fusion.12
  274.0 1.0 copy.28
  (54 shorter events, 6.9 us)
Async XLA Ops:
  7.2 12.0 %copy-start = (bf16[512,2048]{1,0:T(8,128)(2,1)S(1)}, bf16[512,2048]{1,0:T(8,128)(2,1)}, u32[]{:S(2)}) copy-start(bf16[512,2048]{1,0:T(8,128)(2,1)} %param.8) | copy-start | bytes 6291460
  11.8 35.8 %all-to-all-start = ((bf16[8,144,512]{2,1,0:T(8,128)(2,1)}), bf16[8,144,512]{2,1,0:T(8,128)(2,1)S(1)}, u32[]{:S(2)}, u32[]{:S(2)}) async-start(bf16[8,144,512]{2,1,0:T(8,128)(2,1)} %bitcast.55), calls=%async_computation.1 | async-start | bytes 2359296 | tf_op jit(solution)/shard_map/all_to_all | solution.py:13
  47.6 97.1 %all-to-all-start.1 = ((bf16[8,128,2048]{2,1,0:T(8,128)(2,1)}), bf16[8,128,2048]{2,1,0:T(8,128)(2,1)}, u32[]{:S(2)}, u32[]{:S(2)}) async-start(bf16[8,128,2048]{2,1,0:T(8,128)(2,1)} %bitcast.53), calls=%async_computation.2 | async-start | bytes 8388608 | tf_op jit(solution)/shard_map/all_to_all | solution.py:13
  52.2 37.2 %all-reduce.3.cloned.1.call-start = ((), (), s32[]{:S(2)}) async-start(), calls=%async_computation.6 | async-start | bytes 524288 | tf_op jit(solution)/shard_map/psum | solution.py:120
  53.3 1.1 copy-start.3
  53.3 1.2 copy-start.6
  53.3 1.0 copy-start.1
  54.5 2.2 copy-start.4
  54.5 2.3 copy-start.5
  55.9 57.7 %all-gather.2.cloned.1.call-start = ((), (), s32[]{:S(2)}) async-start(), calls=%async_computation.7 | async-start | bytes 2621440 | tf_op jit(solution)/shard_map/all_gather | solution.py:90
  144.7 97.1 %all-to-all-start.2 = ((bf16[8,128,2048]{2,1,0:T(8,128)(2,1)}), bf16[8,128,2048]{2,1,0:T(8,128)(2,1)}, u32[]{:S(2)}, u32[]{:S(2)}) async-start(bf16[8,128,2048]{2,1,0:T(8,128)(2,1)} %bitcast.54), calls=%async_computation.3 | async-start | bytes 8388608 | tf_op jit(solution)/shard_map/all_to_all | solution.py:13
  149.3 111.0 %reduce-scatter.2.cloned.1.call-start = ((), (), s32[]{:S(2)}) async-start(), calls=%async_computation.5 | async-start | bytes 5242880 | tf_op jit(solution)/shard_map/reduce_scatter | solution.py:81
  159.4 19.2 %copy-start.7 = (bf16[8,64,512]{2,1,0:T(8,128)(2,1)S(1)}, bf16[8,64,512]{2,1,0:T(8,128)(2,1)}, u32[]{:S(2)}) copy-start(bf16[8,64,512]{2,1,0:T(8,128)(2,1)} %param.11) | copy-start | bytes 1572868
  180.4 65.7 %copy-start.2 = (bf16[8,128,512]{2,1,0:T(8,128)(2,1)S(1)}, bf16[8,128,512]{2,1,0:T(8,128)(2,1)}, u32[]{:S(2)}) copy-start(bf16[8,128,512]{2,1,0:T(8,128)(2,1)} %copy-done.1) | copy-start | bytes 3145732
  241.8 29.9 %all-to-all-start.3 = ((bf16[8,128,512]{2,1,0:T(8,128)(2,1)}), bf16[8,128,512]{2,1,0:T(8,128)(2,1)}, u32[]{:S(2)}, u32[]{:S(2)}) async-start(bf16[8,128,512]{2,1,0:T(8,128)(2,1)} %bitcast.58), calls=%async_computation.4 | async-start | bytes 2097152 | tf_op jit(solution)/shard_map/all_to_all | solution.py:13
  247.8 6.7 %copy-start.8 = (f32[512,2048]{1,0:T(8,128)S(1)}, f32[512,2048]{1,0:T(8,128)}, u32[]{:S(2)}) copy-start(f32[512,2048]{1,0:T(8,128)} %fusion.35) | copy-start | bytes 12582916
Sparse Core Ops, SparseCore 0:
  56.0 33.2 all-reduce.2
  91.0 22.5 all-gather.1
  159.5 45.5 reduce-scatter.1

commit v3 on v2

--- a/solution.py
+++ b/solution.py
@@ -79,13 +79,11 @@
     input_rows = exchange(send_rows, tok_count)
 
     base_out = lax.psum_scatter(
-        lax.dot_general(
-            frozen_weight, tokens, (((0,), (1,)), ((), ())), preferred_element_type=jnp.float32
-        ),
+        jnp.dot(tokens, frozen_weight, preferred_element_type=jnp.float32),
         "tp",
-        scatter_dimension=0,
+        scatter_dimension=1,
         tiled=True,
-    ).T
+    )
     frozen_input_gradient = lax.dot_general(
         lax.all_gather(output_gradient, "tp", axis=1, tiled=True),
         frozen_weight,

time: 282 us -> 282 us (level)
  no operation moved by 1% of the time
where the time goes in v3:
time: 282 us; the launch traced here: 281 us
  waiting for transfers between devices  168 us (60%)
  matrix products  59.2 us (21%)
  starting transfers between devices  20.9 us (7%)
  between operations  14 us (5%)
  blocking collectives  13.8 us (5%)
  local copies, waits for them, and re-layouts  3 us (1%)
  other arithmetic  2.84 us (1%)
    all_to_all x4, waiting for transfers between devices, exchange(): lax.all_to_all(parts, 'tok', split_axis=0, concat_axis=0, tiled=True)  118 us
    psum x1, waiting for transfers between devices, per_device(): lax.psum(jnp.sum(pull_all * chosen_float[:, :, None], axis=1), 'tp')  31.6 us
    all_to_all x4, starting transfers between devices, exchange(): lax.all_to_all(parts, 'tok', split_axis=0, concat_axis=0, tiled=True)  20.6 us
    all_gather x1, waiting for transfers between devices, per_device(): lax.all_gather(output_gradient, 'tp', axis=1, tiled=True)  17.4 us
    psum x1, blocking collectives, per_device(): lax.psum(jnp.sum(low_all * chosen_float[:, :, None], axis=1), 'tp')  13.8 us
    dot_general x1, matrix products, per_device(): lax.dot_general(lax.all_gather(output_gradient, 'tp', axis=1, tiled=True)...  10.5 us
    dot_general x1, matrix products, per_device(): jnp.dot(tokens, frozen_weight, preferred_element_type=jnp.float32)  9.4 us
    dot_general x1, matrix products, per_device(): jnp.einsum('rd,rak->adk', input_rows, gradient_picked.reshape(row_total,...  6.69 us
  transfers between devices with their start and end apart: 7, of which 6 were waited for; matrix products, arithmetic and copies ran while one was open for 20% of the time, Pallas kernels for 0%

profile of v3, /device:TPU:0, one launch (start us, length us, event | category | flops | bytes accessed | tf_op | source)
XLA Modules:
  0.0 281.3 jit_solution(16071903724552119925)
XLA Ops:
  7.2 1.0 select_reduce_fusion.2
  8.6 3.1 %convolution_convert_fusion.1 = bf16[1152,512]{1,0:T(8,128)(2,1)} fusion(s32[544]{0:T(1024)S(1)} %pad_add_fusion, bf16[32,512]{1,0:T(8,128)(2,1)S(1)} %select_convert_fusion.1, bf16[512,512]{1,0:T(8,128)(2,1)} %param.15), kind=kOutput, calls=%fused_computation.4 | convolution fusion | flops 644059136 | bytes 1738880 | tf_op jit(solution)/shard_map/dot_general | solution.py:68
  11.8 7.3 %all-to-all-start = ((bf16[8,144,512]{2,1,0:T(8,128)(2,1)}), bf16[8,144,512]{2,1,0:T(8,128)(2,1)S(1)}, u32[]{:S(2)}, u32[]{:S(2)}) async-start(bf16[8,144,512]{2,1,0:T(8,128)(2,1)} %bitcast.53), calls=%async_computation.1 | async-start | bytes 2359296 | tf_op jit(solution)/shard_map/all_to_all | solution.py:13
  19.2 4.4 %convolution_convert_fusion = bf16[1024,2048]{1,0:T(8,128)(2,1)} fusion(bf16[512,2048]{1,0:T(8,128)(2,1)S(1)} %copy-done, s32[512]{0:T(512)S(1)} %add.122), kind=kOutput, calls=%fused_computation.2 | convolution fusion | flops 2150105088 | bytes 6293504 | tf_op jit(solution)/shard_map/dot_general | solution.py:78
  23.6 24.1 %all-to-all-done = bf16[8,144,512]{2,1,0:T(8,128)(2,1)S(1)} async-done(((bf16[8,144,512]{2,1,0:T(8,128)(2,1)}), bf16[8,144,512]{2,1,0:T(8,128)(2,1)S(1)}, u32[]{:S(2)}, u32[]{:S(2)}) %all-to-all-start) | async-done | bytes 1179680 | tf_op jit(solution)/shard_map/all_to_all | solution.py:13
  47.6 4.5 %all-to-all-start.1 = ((bf16[8,128,2048]{2,1,0:T(8,128)(2,1)}), bf16[8,128,2048]{2,1,0:T(8,128)(2,1)}, u32[]{:S(2)}, u32[]{:S(2)}) async-start(bf16[8,128,2048]{2,1,0:T(8,128)(2,1)} %bitcast.51), calls=%async_computation.2 | async-start | bytes 8388608 | tf_op jit(solution)/shard_map/all_to_all | solution.py:13
  54.5 1.4 multiply_reduce_fusion
  57.7 31.6 %all-reduce.3.cloned.1.call-done = f32[1024,64]{0,1:T(8,128)} async-done(((f32[1024,64]{0,1:T(8,128)}), f32[1024,64]{0,1:T(8,128)}) %all-reduce.3.cloned.1.call-update) | async-done | bytes 262160 | tf_op jit(solution)/shard_map/psum | solution.py:118
  90.3 5.9 %bitcast_convert_fusion = bf16[1024,2048]{1,0:T(8,128)(2,1)} fusion(bf16[8,2048,64]{1,2,0:T(8,128)(2,1)} %param.10, bf16[1024,64]{0,1:T(8,128)(2,1)S(1)} %multiply_convert_fusion, bf16[1024,8]{0,1:T(8,128)(2,1)S(1)} %convert_element_type.80), kind=kOutput, calls=%fused_computation | convolution fusion | flops 2150105088 | bytes 6438912 | tf_op jit(solution)/shard_map/dot_general | solution.py:125
  96.2 17.4 %all-gather.2.cloned.1.call-done = bf16[512,2048]{1,0:T(8,128)(2,1)} async-done(((bf16[512,512]{1,0:T(8,128)(2,1)}), bf16[512,2048]{1,0:T(8,128)(2,1)}) %all-gather.2.cloned.1.call-update) | async-done | bytes 2097168 | tf_op jit(solution)/shard_map/all_gather | solution.py:88
  113.6 10.5 %fusion.35 = f32[512,2048]{1,0:T(8,128)} fusion(bf16[512,2048]{1,0:T(8,128)(2,1)} %all-gather.2.cloned.1.call-done, bf16[2048,2048]{1,0:T(8,128)(2,1)} %param.9), kind=kOutput, calls=%fused_computation.72 | convolution fusion | flops 4294967296 | bytes 14680064 | tf_op jit(solution)/shard_map/dot_general | solution.py:87
  124.1 20.6 %all-to-all-done.1 = bf16[8,128,2048]{2,1,0:T(8,128)(2,1)} async-done(((bf16[8,128,2048]{2,1,0:T(8,128)(2,1)}), bf16[8,128,2048]{2,1,0:T(8,128)(2,1)}, u32[]{:S(2)}, u32[]{:S(2)}) %all-to-all-start.1) | async-done | bytes 4194336 | tf_op jit(solution)/shard_map/all_to_all | solution.py:13
  144.7 4.6 %all-to-all-start.2 = ((bf16[8,128,2048]{2,1,0:T(8,128)(2,1)}), bf16[8,128,2048]{2,1,0:T(8,128)(2,1)}, u32[]{:S(2)}, u32[]{:S(2)}) async-start(bf16[8,128,2048]{2,1,0:T(8,128)(2,1)} %bitcast.52), calls=%async_computation.3 | async-start | bytes 8388608 | tf_op jit(solution)/shard_map/all_to_all | solution.py:13
  149.6 9.4 %fusion.34 = f32[512,2048]{1,0:T(8,128)} fusion(bf16[512,2048]{1,0:T(8,128)(2,1)S(1)} %copy-done, bf16[2048,2048]{1,0:T(8,128)(2,1)} %param.9), kind=kOutput, calls=%fused_computation.71 | convolution fusion | flops 4294967296 | bytes 14680064 | tf_op jit(solution)/shard_map/dot_general | solution.py:82
  159.0 5.3 %multiply_reduce_fusion.1 = f32[1024,64]{0,1:T(8,128)S(1)} fusion(bf16[1024,2048,1]{1,0,2:T(8,128)(2,1)} %bitcast.3, bf16[8,2048,64]{1,2,0:T(8,128)(2,1)} %param.10, f32[1024,8]{0,1:T(8,128)S(1)} %copy-done.3), kind=kOutput, calls=%fused_computation.12 | convolution fusion | flops 2148466688 | bytes 6586368 | tf_op jit(solution)/shard_map/dot_general | solution.py:133
  164.3 13.8 %all-reduce.4 = bf16[1024,64]{0,1:T(8,128)(2,1)S(1)} all-reduce(f32[1024,64]{0,1:T(8,128)S(1)} %multiply_reduce_fusion.1), channel_id=1, replica_groups=mesh['tok'=8,'tp'=4] {'tp'}, use_global_device_ids=true, to_apply=%region_7.8 | all-reduce | flops 65536 | bytes 393216 | tf_op jit(solution)/shard_map/psum | solution.py:136
  178.2 1.8 fusion
  180.0 61.8 %all-to-all-done.2 = bf16[8,128,2048]{2,1,0:T(8,128)(2,1)} async-done(((bf16[8,128,2048]{2,1,0:T(8,128)(2,1)}), bf16[8,128,2048]{2,1,0:T(8,128)(2,1)}, u32[]{:S(2)}, u32[]{:S(2)}) %all-to-all-start.2) | async-done | bytes 4194336 | tf_op jit(solution)/shard_map/all_to_all | solution.py:13
  241.8 4.2 %all-to-all-start.3 = ((bf16[8,128,512]{2,1,0:T(8,128)(2,1)}), bf16[8,128,512]{2,1,0:T(8,128)(2,1)}, u32[]{:S(2)}, u32[]{:S(2)}) async-start(bf16[8,128,512]{2,1,0:T(8,128)(2,1)} %bitcast.56), calls=%async_computation.4 | async-start | bytes 2097152 | tf_op jit(solution)/shard_map/all_to_all | solution.py:13
  246.1 1.7 convolution_multiply_fusion
  247.8 6.7 %convolution_bitcast_fusion = f32[8,2048,64]{1,2,0:T(8,128)} fusion(bf16[1024,2048,1]{1,0,2:T(8,128)(2,1)} %bitcast.3, bf16[1024,64]{0,1:T(8,128)(2,1)S(1)} %multiply_convert_fusion, bf16[1024,8]{0,1:T(8,128)(2,1)S(1)} %convert_element_type.80), kind=kOutput, calls=%fused_computation.3 | convolution fusion | flops 2148007936 | bytes 8536064 | tf_op jit(solution)/shard_map/rd,rak->adk/dot_general | solution.py:148
  254.5 5.9 %add_convert_fusion = bf16[512,2048]{1,0:T(8,128)(2,1)} fusion(f32[512,2048]{1,0:T(8,128)S(1)} %copy-done.8, bf16[1024,2048]{1,0:T(8,128)(2,1)} %bitcast.10, s32[512]{0:T(512)S(1)} %add.122), kind=kOutput, calls=%fused_computation.1 | convolution fusion | flops 2150105088 | bytes 10487808 | tf_op jit(solution)/shard_map/dot_general | solution.py:161
  260.4 11.3 %all-to-all-done.3 = bf16[8,128,512]{2,1,0:T(8,128)(2,1)} async-done(((bf16[8,128,512]{2,1,0:T(8,128)(2,1)}), bf16[8,128,512]{2,1,0:T(8,128)(2,1)}, u32[]{:S(2)}, u32[]{:S(2)}) %all-to-all-start.3) | async-done | bytes 1048608 | tf_op jit(solution)/shard_map/all_to_all | solution.py:13
  271.7 3.1 %fusion.12 = bf16[512,512]{1,0:T(8,128)(2,1)} fusion(f32[512,512]{1,0:T(8,128)} %reduce-scatter.2.cloned.1.call-done, bf16[1024,512]{1,0:T(8,128)(2,1)} %bitcast.12, s32[512]{0:T(512)S(1)} %add.122), kind=kOutput, calls=%fused_computation.22 | convolution fusion | flops 537919488 | bytes 2623488 | tf_op jit(solution)/shard_map/dot_general | solution.py:164
  (53 shorter events, 5.9 us)
Async XLA Ops:
  7.2 12.0 %copy-start = (bf16[512,2048]{1,0:T(8,128)(2,1)S(1)}, bf16[512,2048]{1,0:T(8,128)(2,1)}, u32[]{:S(2)}) copy-start(bf16[512,2048]{1,0:T(8,128)(2,1)} %param.8) | copy-start | bytes 6291460
  11.8 35.8 %all-to-all-start = ((bf16[8,144,512]{2,1,0:T(8,128)(2,1)}), bf16[8,144,512]{2,1,0:T(8,128)(2,1)S(1)}, u32[]{:S(2)}, u32[]{:S(2)}) async-start(bf16[8,144,512]{2,1,0:T(8,128)(2,1)} %bitcast.53), calls=%async_computation.1 | async-start | bytes 2359296 | tf_op jit(solution)/shard_map/all_to_all | solution.py:13
  47.6 97.1 %all-to-all-start.1 = ((bf16[8,128,2048]{2,1,0:T(8,128)(2,1)}), bf16[8,128,2048]{2,1,0:T(8,128)(2,1)}, u32[]{:S(2)}, u32[]{:S(2)}) async-start(bf16[8,128,2048]{2,1,0:T(8,128)(2,1)} %bitcast.51), calls=%async_computation.2 | async-start | bytes 8388608 | tf_op jit(solution)/shard_map/all_to_all | solution.py:13
  52.2 37.2 %all-reduce.3.cloned.1.call-start = ((), (), s32[]{:S(2)}) async-start(), calls=%async_computation.6 | async-start | bytes 524288 | tf_op jit(solution)/shard_map/psum | solution.py:118
  53.3 1.1 copy-start.3
  53.3 1.2 copy-start.6
  53.3 1.0 copy-start.1
  54.5 2.2 copy-start.4
  54.5 2.3 copy-start.5
  55.9 57.7 %all-gather.2.cloned.1.call-start = ((), (), s32[]{:S(2)}) async-start(), calls=%async_computation.7 | async-start | bytes 2621440 | tf_op jit(solution)/shard_map/all_gather | solution.py:88
  144.7 97.1 %all-to-all-start.2 = ((bf16[8,128,2048]{2,1,0:T(8,128)(2,1)}), bf16[8,128,2048]{2,1,0:T(8,128)(2,1)}, u32[]{:S(2)}, u32[]{:S(2)}) async-start(bf16[8,128,2048]{2,1,0:T(8,128)(2,1)} %bitcast.52), calls=%async_computation.3 | async-start | bytes 8388608 | tf_op jit(solution)/shard_map/all_to_all | solution.py:13
  149.3 111.0 %reduce-scatter.2.cloned.1.call-start = ((), (), s32[]{:S(2)}) async-start(), calls=%async_computation.5 | async-start | bytes 5242880 | tf_op jit(solution)/shard_map/reduce_scatter | solution.py:81
  159.0 19.2 %copy-start.7 = (bf16[8,64,512]{2,1,0:T(8,128)(2,1)S(1)}, bf16[8,64,512]{2,1,0:T(8,128)(2,1)}, u32[]{:S(2)}) copy-start(bf16[8,64,512]{2,1,0:T(8,128)(2,1)} %param.11) | copy-start | bytes 1572868
  180.0 66.1 %copy-start.2 = (bf16[8,128,512]{2,1,0:T(8,128)(2,1)S(1)}, bf16[8,128,512]{2,1,0:T(8,128)(2,1)}, u32[]{:S(2)}) copy-start(bf16[8,128,512]{2,1,0:T(8,128)(2,1)} %copy-done.1) | copy-start | bytes 3145732
  241.8 29.9 %all-to-all-start.3 = ((bf16[8,128,512]{2,1,0:T(8,128)(2,1)}), bf16[8,128,512]{2,1,0:T(8,128)(2,1)}, u32[]{:S(2)}, u32[]{:S(2)}) async-start(bf16[8,128,512]{2,1,0:T(8,128)(2,1)} %bitcast.56), calls=%async_computation.4 | async-start | bytes 2097152 | tf_op jit(solution)/shard_map/all_to_all | solution.py:13
  247.8 6.7 %copy-start.8 = (f32[512,2048]{1,0:T(8,128)S(1)}, f32[512,2048]{1,0:T(8,128)}, u32[]{:S(2)}) copy-start(f32[512,2048]{1,0:T(8,128)} %fusion.35) | copy-start | bytes 12582916
Sparse Core Ops, SparseCore 0:
  56.0 33.2 all-reduce.2
  91.0 22.5 all-gather.1
  159.1 45.5 reduce-scatter.1
